TPU v7x, 32 devices: a whole 2x2x4 slice. The times are simulated.
32 devices in a mesh: row: 16 (over z, y, core), col: 2 (over x).
Axes of the slice: x: 2, y: 2, z: 4, core: 2. Of those that a mesh axis runs over, the one named last changes fastest.
Arguments:
- pair_prefactor: bfloat16 [4, 10240, 10240], P(None, 'row', 'col'), may hold values from -6 to 6
- boys_argument: bfloat16 [4, 10240, 10240], P(None, 'row', 'col'), may hold values from 1 to 4
- orbitals: bfloat16 [10240, 1024], P('col', 'row'), may hold values from -0.0625 to 0.0625
- screen_mask: int32 [80, 80], replicated, may hold values 0 or 1
- momentum: int32 [80], replicated, may hold values from 0 to 3
Outputs:
- exchange_matrix: float32 [10240, 10240], P('row', 'col')
Inputs may be any that keep to these rules, and one draw needn't show every extreme that they name: `screen_mask`: 1 where the block pair passes screening, else 0. One angular momentum for each block of 128 basis functions.
All inputs are finite; a program needn't handle non-finite values.
Results may differ from a plain program's by a relative error of at most 0.0047.
Values may be sent and summed in bfloat16 or wider, within the bound.
A program may use at most 192 MiB of HBM per device.

v0:
```python
import math

import jax
import jax.numpy as jnp
from jax import lax
from jax.sharding import PartitionSpec as P

NOCC = 1024
BLK = 128
MAXL = 3
AUX = 4


def boys_value(argument, order):
    decay = jnp.exp(-argument)
    current = 0.5 * jnp.sqrt(jnp.pi / argument) * jax.scipy.special.erf(jnp.sqrt(argument))
    chosen = jnp.where(order == 0, current, jnp.zeros_like(current))
    for level in range(2 * MAXL):
        current = ((2.0 * level + 1.0) * current - decay) / (2.0 * argument)
        chosen = jnp.where(order == level + 1, current, chosen)
    return chosen


def tile_values(prefactor, argument, order, screen):
    argument_full = argument.astype(jnp.float32)
    factor = (2 * order + 1).astype(jnp.float32) * boys_value(argument_full, order)
    return (prefactor.astype(jnp.float32) * factor * screen).astype(jnp.bfloat16)


def body(pair_prefactor, boys_argument, orbitals, screen_mask, momentum):
    mine_rows = pair_prefactor.shape[1]
    mine_cols = pair_prefactor.shape[2]
    blocks_all = momentum.shape[0]
    row_index = lax.axis_index("row")
    col_index = lax.axis_index("col")
    global_rows = row_index * mine_rows + lax.iota(jnp.int32, mine_rows)
    member = global_rows[:, None] // BLK == lax.iota(jnp.int32, blocks_all)[None, :]
    row_order = jnp.sum(jnp.where(member, momentum[None, :], 0), axis=1)
    row_screen = jnp.dot(
        member.astype(jnp.float32),
        screen_mask.astype(jnp.float32),
        preferred_element_type=jnp.float32,
    )
    col_blocks = mine_cols // BLK
    col_screen = lax.dynamic_slice_in_dim(row_screen, col_index * col_blocks, col_blocks, 1)
    screen_tile = jnp.repeat(col_screen, BLK, axis=1)
    col_order = jnp.repeat(
        lax.dynamic_slice_in_dim(momentum, col_index * col_blocks, col_blocks, 0), BLK
    )
    order_sum = row_order[:, None] + col_order[None, :]
    tile_vals = tile_values(pair_prefactor, boys_argument, order_sum[None], screen_tile[None])
    coeff_all = lax.all_gather(orbitals, "row", axis=1, tiled=True)
    partial_panel = jnp.einsum(
        "pmn,nk->pmk", tile_vals, coeff_all, preferred_element_type=jnp.float32
    )
    half_panel = lax.psum_scatter(partial_panel, "col", scatter_dimension=2, tiled=True).astype(
        jnp.bfloat16
    )
    scale_factor = 1.0 / math.sqrt(AUX * NOCC)
    wide_part = jnp.einsum(
        "pmk,pnk->mn",
        half_panel,
        lax.all_gather(half_panel, "row", axis=1, tiled=True),
        preferred_element_type=jnp.float32,
    )
    summed = lax.psum_scatter(wide_part, "col", scatter_dimension=1, tiled=True)
    return summed * scale_factor


def solution(mesh):
    placed = (P(None, "row", "col"), P(None, "row", "col"), P("col", "row"), P(), P())
    return jax.shard_map(
        body, mesh=mesh, in_specs=placed, out_specs=P("row", "col"), check_vma=False
    )
```

profile of v0, /device:TPU:0, one launch (start us, length us, event | category | flops | bytes accessed | tf_op | source)
XLA Modules:
  0.0 933.3 jit_solution(6177169209032267751)
XLA Ops:
  6.5 0.0 all-gather.3.cloned.1.call-start
  6.5 0.7 all-gather.3.cloned.1.call-update
  7.3 0.0 reduce-scatter.3.cloned.1.call-start
  7.3 0.7 dynamic_slice.6
  8.1 1.0 fusion.25
  9.1 0.2 copy.7
  9.2 7.2 broadcast_in_dim.75
  16.4 0.0 copy-start
  16.4 12.8 %copy.10 = f32[80,8,40,128]{3,1,2,0:T(8,128)} copy(f32[80,8,40,128]{3,2,1,0:T(8,128)} %bitcast.14) | data formatting | bytes 26214400
  29.2 0.0 copy-done
  29.2 0.1 select_reduce_fusion
  29.3 0.1 broadcast_bitcast_fusion
  29.4 7.1 fusion.23
  36.5 14.9 %add_compare_fusion.6 = (pred[640,5120]{1,0:T(8,128)(4,1)S(1)}, pred[640,5120]{1,0:T(8,128)(4,1)}, pred[640,5120]{1,0:T(8,128)(4,1)}, pred[640,5120]{1,0:T(8,128...) fusion(s32[5120]{0:T(1024)S(1)} %broadcast_bitcast_fusion, ...), kind=kLoop, calls=%fused_computation.16 | loop fusion | flops 26214400 | bytes 22960640 | tf_op jit(solution)/shard_map/eq | solution.py:20
  51.4 48.8 %all-gather.3.cloned.1.call-done = bf16[5120,1024]{0,1:T(8,128)(2,1)} async-done(((bf16[5120,64]{0,1:T(8,128)(2,1)}), bf16[5120,1024]{0,1:T(8,128)(2,1)}) %all-gather.3.cloned.1.call-update) | async-done | bytes 10485776 | tf_op jit(solution)/shard_map/all_gather | solution.py:52
  100.3 156.4 %fusion.20 = f32[4,640,1024]{2,1,0:T(8,128)} fusion(bf16[4,640,5120]{2,1,0:T(8,128)(2,1)} %param.6, bf16[4,640,5120]{2,1,0:T(8,128)(2,1)} %param.5, f32[640,5120]{1,0:T(8,128)} %bitcast.15, f32[640,5120]{1,0:T(8,128)} %fusion.23, pred[640,5120]{1,0:T(8,128)(4,1)} %get-tuple-element.6, pred[640,5120]{1,0:T(8,128)(4,1)} %get-tuple-element.7, ...), kind=kOutput, calls=%fused_computation.33 | convolution fusion | flops 27302297600 | bytes 122552320 | tf_op jit(solution)/shard_map/pmn,nk->pmk/dot_general | solution.py:53
  256.7 0.0 reduce-scatter.3.cloned.1.call-update
  256.7 0.0 all-gather.5.cloned.1.call-start
  256.7 120.1 %reduce-scatter.3.cloned.1.call-done = f32[4,640,512]{2,1,0:T(8,128)} async-done(((f32[4,640,1024]{2,1,0:T(8,128)}), f32[4,640,512]{2,1,0:T(8,128)}) %reduce-scatter.3.cloned.1.call-update) | async-done | bytes 5242896 | tf_op jit(solution)/shard_map/reduce_scatter | solution.py:56
  376.9 4.3 convert_element_type.29
  381.2 0.0 all-gather.5.cloned.1.call-update
  381.2 0.0 reduce-scatter.5.cloned.1.call-start
  381.3 207.7 %all-gather.5.cloned.1.call-done = bf16[4,10240,512]{2,1,0:T(8,128)(2,1)} async-done(((bf16[4,640,512]{2,1,0:T(8,128)(2,1)}), bf16[4,10240,512]{2,1,0:T(8,128)(2,1)}) %all-gather.5.cloned.1.call-update) | async-done | bytes 41943056 | tf_op jit(solution)/shard_map/all_gather | solution.py:63
  589.0 35.3 %convolution_bitcast_fusion = f32[640,10240]{1,0:T(8,128)} fusion(bf16[4,640,512]{2,1,0:T(8,128)(2,1)} %convert_element_type.29, bf16[4,10240,512]{2,1,0:T(8,128)(2,1)} %all-gather.5.cloned.1.call-done), kind=kOutput, calls=%fused_computation.34 | convolution fusion | flops 26843545600 | bytes 70778880 | tf_op jit(solution)/shard_map/pmk,pnk->mn/dot_general | solution.py:60
  624.3 0.0 reduce-scatter.5.cloned.1.call-update
  624.3 290.7 %reduce-scatter.5.cloned.1.call-done = f32[640,5120]{1,0:T(8,128)} async-done(((f32[640,10240]{1,0:T(8,128)}), f32[640,5120]{1,0:T(8,128)}) %reduce-scatter.5.cloned.1.call-update) | async-done | bytes 13107216 | tf_op jit(solution)/shard_map/reduce_scatter | solution.py:66
  915.0 11.8 %broadcast_multiply_fusion = f32[640,5120]{1,0:T(8,128)} fusion(f32[640,5120]{1,0:T(8,128)} %reduce-scatter.5.cloned.1.call-done), kind=kLoop, calls=%fused_computation.39 | loop fusion | flops 3276800 | bytes 26214400 | tf_op jit(solution)/shard_map/mul | solution.py:67
  (2 shorter events, 0.0 us)
Async XLA Ops:
  6.5 93.7 %all-gather.3.cloned.1.call-start = ((), (), s32[]{:S(2)}) async-start(), calls=%async_computation.2 | async-start | bytes 11141120 | tf_op jit(solution)/shard_map/all_gather | solution.py:52
  7.3 369.6 %reduce-scatter.3.cloned.1.call-start = ((), (), s32[]{:S(2)}) async-start(), calls=%async_computation.3 | async-start | bytes 15728640 | tf_op jit(solution)/shard_map/reduce_scatter | solution.py:56
  16.4 12.8 %copy-start = (s32[80]{0:T(128)S(1)}, s32[80]{0:T(128)}, u32[]{:S(2)}) copy-start(s32[80]{0:T(128)} %param.9) | copy-start | bytes 964
  256.7 332.3 %all-gather.5.cloned.1.call-start = ((), (), s32[]{:S(2)}) async-start(), calls=%async_computation.4 | async-start | bytes 44564480 | tf_op jit(solution)/shard_map/all_gather | solution.py:63
  381.2 533.8 %reduce-scatter.5.cloned.1.call-start = ((), (), s32[]{:S(2)}) async-start(), calls=%async_computation.5 | async-start | bytes 39321600 | tf_op jit(solution)/shard_map/reduce_scatter | solution.py:66
Sparse Core Ops, SparseCore 0:
  9.6 90.5 all-gather.2
  256.8 120.0 reduce-scatter.2
  381.3 207.5 all-gather.4
  624.4 290.5 reduce-scatter.4
where the time goes:
time: 934 us; the launch traced here: 933 us
  waiting for transfers between devices  668 us (72%)
  matrix products  193 us (21%)
  other arithmetic  38.2 us (4%)
  local copies, waits for them, and re-layouts  21 us (2%)
  between operations  13.2 us (1%)
    reduce_scatter x1, waiting for transfers between devices, body(): summed = lax.psum_scatter(wide_part, 'col', scatter_dimension=1, tiled=True)  291 us
    all_gather x1, waiting for transfers between devices, body(): lax.all_gather(half_panel, 'row', axis=1, tiled=True)  208 us
    dot_general x1, matrix products, body(): jnp.einsum('pmn,nk->pmk', tile_vals, coeff_all, preferred_element_type=jn...  156 us
    reduce_scatter x1, waiting for transfers between devices, body(): lax.psum_scatter(partial_panel, 'col', scatter_dimension=2, tiled=True)  120 us
    all_gather x1, waiting for transfers between devices, body(): coeff_all = lax.all_gather(orbitals, 'row', axis=1, tiled=True)  48.8 us
    dot_general x1, matrix products, body(): jnp.einsum('pmk,pnk->mn', half_panel, lax.all_gather(half_panel, 'row', a...  35.3 us
  transfers between devices with their start and end apart: 4, of which 4 were waited for; matrix products, arithmetic and copies ran while one was open for 5% of the time, Pallas kernels for 0%

commit v1 on v0

v1 whole, which is shorter than its diff:
```python
import functools
import math

import jax
import jax.numpy as jnp
from jax import lax
from jax.experimental import pallas as pl
from jax.experimental.pallas import tpu as pltpu
from jax.sharding import PartitionSpec as P

NOCC = 1024
BLK = 128
AUX = 4
CHUNKS = 5
SUB = 64


def tile_kernel(first, order_ref, screen_ref, pre_ref, arg_ref, out_ref):
    span = pre_ref.shape[2] // BLK
    row = first + pl.program_id(0)
    start = pl.program_id(1) * span

    for p in range(pre_ref.shape[0]):
        for b in range(span):
            order = order_ref[row, start + b]
            cols = pl.ds(b * BLK, BLK)

            @pl.when(screen_ref[row, start + b] == 0)
            def _():
                out_ref[p, :, cols] = jnp.zeros((SUB, BLK), out_ref.dtype)

            @pl.when(screen_ref[row, start + b] != 0)
            def _():
                t = arg_ref[p, :, cols].astype(jnp.float32)
                decay = jnp.exp(-t)
                inverse_root = lax.rsqrt(t)
                half_inverse = 0.5 * inverse_root * inverse_root
                value = (0.5 * math.sqrt(math.pi)) * inverse_root * lax.erf(t * inverse_root)

                def step(level, value):
                    odd = (2 * level + 1).astype(jnp.float32)
                    return (odd * value - decay) * half_inverse

                value = lax.fori_loop(0, order, step, value)
                weight = (2 * order + 1).astype(jnp.float32)
                pre = pre_ref[p, :, cols].astype(jnp.float32)
                out_ref[p, :, cols] = (pre * (weight * value)).astype(out_ref.dtype)


def tile_chunk(pair_prefactor, boys_argument, order, screen, chunk, height):
    aux, _, width = pair_prefactor.shape
    first = chunk * height // SUB
    wide = width // 2
    spec = pl.BlockSpec((aux, SUB, wide), lambda i, j, *_: (0, first + i, j))
    return pl.pallas_call(
        functools.partial(tile_kernel, first),
        out_shape=jax.ShapeDtypeStruct((aux, height, width), jnp.bfloat16),
        grid_spec=pltpu.PrefetchScalarGridSpec(
            num_scalar_prefetch=2,
            grid=(height // SUB, width // wide),
            in_specs=[spec, spec],
            out_specs=pl.BlockSpec((aux, SUB, wide), lambda i, j, *_: (0, i, j)),
        ),
        compiler_params=pltpu.CompilerParams(vmem_limit_bytes=32 << 20),
        cost_estimate=pl.CostEstimate(
            flops=60 * aux * height * width,
            bytes_accessed=6 * aux * height * width,
            transcendentals=3 * aux * height * width,
        ),
    )(order, screen, pair_prefactor, boys_argument)


def assemble_kernel(height, per, scale, *refs):
    own, received, out_ref = refs[:CHUNKS], refs[CHUNKS:-1], refs[-1]
    extra = len(received) // CHUNKS
    for chunk in range(CHUNKS):
        total = own[chunk][...]
        for part in received[chunk * extra : (chunk + 1) * extra]:
            total = total + part[...].astype(jnp.float32)
        total = total * scale
        for s in range(per):
            at = s * CHUNKS * height + chunk * height
            out_ref[:, at : at + height] = total[:, s * height : (s + 1) * height]


def assemble(own, received, height, per, scale):
    rows, span = own[0].shape
    spec = pl.BlockSpec((SUB, span), lambda i: (i, 0))
    return pl.pallas_call(
        functools.partial(assemble_kernel, height, per, scale),
        out_shape=jax.ShapeDtypeStruct((rows, CHUNKS * span), jnp.float32),
        grid=(rows // SUB,),
        in_specs=[spec] * (len(own) + len(received)),
        out_specs=pl.BlockSpec((SUB, CHUNKS * span), lambda i: (i, 0)),
        compiler_params=pltpu.CompilerParams(vmem_limit_bytes=32 << 20),
    )(*own, *received)


def body(cols, pair_prefactor, boys_argument, orbitals, screen_mask, momentum):
    mine_rows, mine_cols = pair_prefactor.shape[1:]
    row_index = lax.axis_index("row")
    col_index = lax.axis_index("col")
    height = mine_rows // CHUNKS
    share = NOCC // cols
    per = mine_cols // mine_rows
    span = per * height
    scale = 1.0 / math.sqrt(AUX * NOCC)

    coeff_all = lax.all_gather(orbitals, "row", axis=1, tiled=True)

    row_blocks = (row_index * mine_rows + SUB * lax.iota(jnp.int32, mine_rows // SUB)) // BLK
    col_blocks = col_index * (mine_cols // BLK) + lax.iota(jnp.int32, mine_cols // BLK)
    order = momentum[row_blocks][:, None] + momentum[col_blocks][None, :]
    screen = screen_mask[row_blocks][:, col_blocks]

    peers = [lax.rem(col_index + k, cols) for k in range(cols)]
    coeff = [lax.dynamic_slice_in_dim(coeff_all, peer * share, share, 1) for peer in peers]
    paths = [[(i, (i + k) % cols) for i in range(cols)] for k in range(cols)]

    def project(tile, part):
        return jnp.einsum("pmn,nk->pmk", tile, part, preferred_element_type=jnp.float32)

    shares, panels, tiles = [], [], []
    for chunk in range(CHUNKS):
        if chunk >= 2:
            order = lax.optimization_barrier((order, shares[chunk - 2]))[0]
        tiles.append(tile_chunk(pair_prefactor, boys_argument, order, screen, chunk, height))
        tile = tiles[-1]
        if chunk >= 1:
            tile = lax.optimization_barrier((tile, shares[chunk - 1]))[0]
        received = [
            lax.ppermute(project(tile, coeff[k]).astype(jnp.bfloat16), "col", paths[k])
            for k in range(1, cols)
        ]
        total = lax.optimization_barrier(project(tile, coeff[0]))
        for part in received:
            total = total + part.astype(jnp.float32)
        shares.append(total.astype(jnp.bfloat16))
        panels.append(lax.all_gather(shares[-1], "row", axis=1, tiled=True))

    mine = jnp.concatenate(shares, axis=1)

    def product(panel, peer):
        other = lax.dynamic_slice_in_dim(panel, peer * span, span, 1)
        return jnp.einsum("pmk,pnk->mn", mine, other, preferred_element_type=jnp.float32)

    own, received = [], []
    for chunk, panel in enumerate(panels):
        if chunk:
            panel = lax.optimization_barrier((panel, own[-1]))[0]
        received += [
            lax.ppermute(product(panel, peers[k]).astype(jnp.bfloat16), "col", paths[k])
            for k in range(1, cols)
        ]
        own.append(lax.optimization_barrier(product(panel, peers[0])))
    return assemble(own, received, height, per, scale)


def solution(mesh):
    placed = (P(None, "row", "col"), P(None, "row", "col"), P("col", "row"), P(), P())
    return jax.shard_map(
        functools.partial(body, mesh.shape["col"]),
        mesh=mesh, in_specs=placed, out_specs=P("row", "col"), check_vma=False,
    )
```

time: 934 us -> 559 us (0.60)
  waiting for transfers between devices: 668 us -> 299 us
  Pallas kernels: 0 us -> 105 us
  matrix products: 193 us -> 105 us
  other arithmetic: 38.2 us -> 5.03 us
  starting transfers between devices: 0.13 us -> 14.6 us
  local copies, waits for them, and re-layouts: 21 us -> 8.26 us
    reduce_scatter x2 -> x0, waiting for transfers between devices: 411 us -> none  [the longest x1 291 us: body(): summed = lax.psum_scatter(wide_part, 'col', scatter_dimension=1, tiled=True)]
    pallas_call x0 -> x6, Pallas kernels: none -> 105 us  [the longest x5 95.4 us: tile_chunk(): pl.pallas_call(functools.partial(tile_kernel, first), out_shape=jax.Shape...]
    dot_general x3 -> x20, matrix products: 193 us -> 105 us  [the longest x10 53.8 us: product(): jnp.einsum('pmk,pnk->mn', mine, other, preferred_element_type=jnp.float32)]
    ppermute x0 -> x10, waiting for transfers between devices: none -> 61.9 us  [the longest x5 35.4 us: body(): lax.ppermute(project(tile, coeff[k]).astype(jnp.bfloat16), 'col', paths[k])]
    all_gather x1 -> x5, waiting for transfers between devices: 208 us -> 168 us  [body(): panels.append(lax.all_gather(shares[-1], 'row', axis=1, tiled=True))]
    all_gather x1, waiting for transfers between devices: 48.8 us -> 68 us  [body(): coeff_all = lax.all_gather(orbitals, 'row', axis=1, tiled=True)]
    eq x1 -> x0, other arithmetic: 14.9 us -> none  [boys_value(): chosen = jnp.where(order == level + 1, current, chosen)]
    ppermute x0 -> x10, starting transfers between devices: none -> 13 us  [the longest x5 6.55 us: body(): lax.ppermute(project(tile, coeff[k]).astype(jnp.bfloat16), 'col', paths[k])]
  transfers between devices with their start and end apart: 4 -> 16, of which waited for: 4 -> 10; matrix products, arithmetic and copies ran while one was open for 5% -> 19% of each run, Pallas kernels for 0% -> 17%
where the time goes in v1:
time: 559 us; the launch traced here: 551 us
  waiting for transfers between devices  299 us (53%)
  Pallas kernels  105 us (19%)
  matrix products  105 us (19%)
  starting transfers between devices  14.6 us (3%)
  between operations  14 us (3%)
  local copies, waits for them, and re-layouts  8.26 us (1%)
    all_gather x5, waiting for transfers between devices, body(): panels.append(lax.all_gather(shares[-1], 'row', axis=1, tiled=True))  168 us
    pallas_call x5, Pallas kernels, tile_chunk(): pl.pallas_call(functools.partial(tile_kernel, first), out_shape=jax.Shape...  95.4 us
    all_gather x1, waiting for transfers between devices, body(): coeff_all = lax.all_gather(orbitals, 'row', axis=1, tiled=True)  68 us
    dot_general x10, matrix products, product(): jnp.einsum('pmk,pnk->mn', mine, other, preferred_element_type=jnp.float32)  53.8 us
    dot_general x10, matrix products, project(): jnp.einsum('pmn,nk->pmk', tile, part, preferred_element_type=jnp.float32)  51.7 us
    ppermute x5, waiting for transfers between devices, body(): lax.ppermute(project(tile, coeff[k]).astype(jnp.bfloat16), 'col', paths[k])  35.4 us
    ppermute x5, waiting for transfers between devices, body(): lax.ppermute(product(panel, peers[k]).astype(jnp.bfloat16), 'col', paths[k])  26.5 us
  transfers between devices with their start and end apart: 16, of which 10 were waited for; matrix products, arithmetic and copies ran while one was open for 19% of the time, Pallas kernels for 17%

profile of v1, /device:TPU:0, one launch (start us, length us, event | category | flops | bytes accessed | tf_op | source)
XLA Modules:
  0.0 551.3 jit_solution(343021442654715957)
XLA Ops:
  6.5 0.7 all-gather.7.cloned.1.call-update
  7.4 1.4 gather_fusion.1
  8.8 1.3 gather_fusion
  10.1 0.6 gather_fusion.2
  10.7 0.1 copy.12
  10.8 0.6 gather_fusion.3
  11.4 0.1 copy.13
  11.5 18.4 %shard_map.55 = bf16[4,128,5120]{2,1,0:T(8,128)(2,1)S(1)} custom-call(s32[10,40]{1,0:T(8,128)S(1)} %broadcast_add_fusion.order_ref, s32[10,40]{1,0:T(8,128)S(1)} %bitcast.87, bf16[4,640,5120]{2,1,0:T(8,128)(2,1)} %pre_ref.9, bf16[4,640,5120]{2,1,0:T(8,128)(2,1)} %arg_ref.9), custom_call_target="tpu_custom_call" | custom-call | flops 157286400 | bytes 15728640 | tf_op jit(solution)/shard_map/pallas_call | solution.py:55
  29.9 2.3 copy-done.2
  32.3 68.0 %all-gather.7.cloned.1.call-done = bf16[5120,1024]{0,1:T(8,128)(2,1)} async-done(((bf16[5120,64]{0,1:T(8,128)(2,1)}), bf16[5120,1024]{0,1:T(8,128)(2,1)}) %all-gather.7.cloned.1.call-update) | async-done | bytes 10485776 | tf_op jit(solution)/shard_map/all_gather | solution.py:109
  100.3 7.1 %fusion.75 = bf16[4,128,512]{2,1,0:T(8,128)(2,1)S(1)} fusion(bf16[4,128,5120]{2,1,0:T(8,128)(2,1)} %copy-done.2, bf16[5120,1024]{0,1:T(8,128)(2,1)} %all-gather.7.cloned.1.call-done, s32[]{:T(128)S(6)} %select_n.58), kind=kOutput, calls=%fused_computation.64 | convolution fusion | flops 2684616704 | bytes 11010052 | tf_op jit(solution)/shard_map/pmn,nk->pmk/dot_general | solution.py:121
  107.4 1.5 collective-permute-start
  108.9 2.9 fusion.18
  111.8 9.7 %collective-permute-done = bf16[4,128,512]{2,1,0:T(8,128)(2,1)S(1)} collective-permute-done((bf16[4,128,512]{2,1,0:T(8,128)(2,1)S(1)}, bf16[4,128,512]{2,1,0:T(8,128)(2,1)S(1)}, u32[]{:S(2)}, u32[]{:S(2)}) %collective-permute-start) | collective-permute-done | bytes 524320 | tf_op jit(solution)/shard_map/ppermute | solution.py:132
  121.5 1.0 constant_dynamic-update-slice_fusion.4
  122.5 0.6 all-gather.11.cloned.1.call-start
  123.1 18.3 %shard_map.56 = bf16[4,128,5120]{2,1,0:T(8,128)(2,1)S(1)} custom-call(s32[10,40]{1,0:T(8,128)S(1)} %broadcast_add_fusion.order_ref, s32[10,40]{1,0:T(8,128)S(1)} %bitcast.88, bf16[4,640,5120]{2,1,0:T(8,128)(2,1)} %pre_ref.9, bf16[4,640,5120]{2,1,0:T(8,128)(2,1)} %arg_ref.9), custom_call_target="tpu_custom_call" | custom-call | flops 157286400 | bytes 15728640 | tf_op jit(solution)/shard_map/pallas_call | solution.py:55
  141.4 5.4 fusion.78
  146.9 1.3 collective-permute-start.1
  148.2 5.0 fusion.16
  153.2 7.5 %collective-permute-done.1 = bf16[4,128,512]{2,1,0:T(8,128)(2,1)S(1)} collective-permute-done((bf16[4,128,512]{2,1,0:T(8,128)(2,1)S(1)}, bf16[4,128,512]{2,1,0:T(8,128)(2,1)S(1)}, u32[]{:S(2)}, u32[]{:S(2)}) %collective-permute-start.1) | collective-permute-done | bytes 524320 | tf_op jit(solution)/shard_map/ppermute | solution.py:132
  160.7 1.0 constant_dynamic-update-slice_fusion.3
  161.7 0.2 all-gather.13.cloned.1.call-start
  162.0 19.8 %shard_map.57 = bf16[4,128,5120]{2,1,0:T(8,128)(2,1)S(1)} custom-call(s32[10,40]{1,0:T(8,128)S(1)} %broadcast_add_fusion.order_ref, s32[10,40]{1,0:T(8,128)S(1)} %bitcast.89, bf16[4,640,5120]{2,1,0:T(8,128)(2,1)} %pre_ref.9, bf16[4,640,5120]{2,1,0:T(8,128)(2,1)} %arg_ref.9), custom_call_target="tpu_custom_call" | custom-call | flops 157286400 | bytes 15728640 | tf_op jit(solution)/shard_map/pallas_call | solution.py:55
  181.7 5.4 fusion.81
  187.1 0.8 collective-permute-start.2
  187.9 5.0 fusion.14
  192.9 8.3 %collective-permute-done.2 = bf16[4,128,512]{2,1,0:T(8,128)(2,1)S(1)} collective-permute-done((bf16[4,128,512]{2,1,0:T(8,128)(2,1)S(1)}, bf16[4,128,512]{2,1,0:T(8,128)(2,1)S(1)}, u32[]{:S(2)}, u32[]{:S(2)}) %collective-permute-start.2) | collective-permute-done | bytes 524320 | tf_op jit(solution)/shard_map/ppermute | solution.py:132
  201.2 1.0 constant_dynamic-update-slice_fusion.2
  202.2 0.3 all-gather.15.cloned.1.call-start
  202.5 18.6 %shard_map.58 = bf16[4,128,5120]{2,1,0:T(8,128)(2,1)S(1)} custom-call(s32[10,40]{1,0:T(8,128)S(1)} %broadcast_add_fusion.order_ref, s32[10,40]{1,0:T(8,128)S(1)} %bitcast.90, bf16[4,640,5120]{2,1,0:T(8,128)(2,1)} %pre_ref.9, bf16[4,640,5120]{2,1,0:T(8,128)(2,1)} %arg_ref.9), custom_call_target="tpu_custom_call" | custom-call | flops 157286400 | bytes 15728640 | tf_op jit(solution)/shard_map/pallas_call | solution.py:55
  221.1 5.4 fusion.84
  226.5 0.1 collective-permute-start.3
  226.6 5.0 fusion.12
  231.6 7.7 %collective-permute-done.3 = bf16[4,128,512]{2,1,0:T(8,128)(2,1)S(1)} collective-permute-done((bf16[4,128,512]{2,1,0:T(8,128)(2,1)S(1)}, bf16[4,128,512]{2,1,0:T(8,128)(2,1)S(1)}, u32[]{:S(2)}, u32[]{:S(2)}) %collective-permute-start.3) | collective-permute-done | bytes 524320 | tf_op jit(solution)/shard_map/ppermute | solution.py:132
  239.3 1.0 constant_dynamic-update-slice_fusion.1
  240.3 0.4 all-gather.17.cloned.1.call-start
  240.8 20.3 %shard_map.59 = bf16[4,128,5120]{2,1,0:T(8,128)(2,1)S(1)} custom-call(s32[10,40]{1,0:T(8,128)S(1)} %broadcast_add_fusion.order_ref, s32[10,40]{1,0:T(8,128)S(1)} %bitcast.91, bf16[4,640,5120]{2,1,0:T(8,128)(2,1)} %pre_ref.9, bf16[4,640,5120]{2,1,0:T(8,128)(2,1)} %arg_ref.9), custom_call_target="tpu_custom_call" | custom-call | flops 157286400 | bytes 15728640 | tf_op jit(solution)/shard_map/pallas_call | solution.py:55
  261.1 5.5 fusion.87
  266.6 2.8 collective-permute-start.4
  269.4 5.1 fusion.10
  274.5 2.1 collective-permute-done.4
  276.5 1.0 constant_dynamic-update-slice_fusion
  277.6 1.4 copy-done.7
  279.0 6.1 %fusion.50.refs_0_ = f32[640,1024]{1,0:T(8,128)S(1)} fusion(bf16[4,640,512]{2,1,0:T(8,128)(2,1)} %copy-done.7, bf16[4,2048,512]{2,1,0:T(8,128)(2,1)} %all-gather.9.cloned.1.call-done, s32[]{:T(128)S(6)} %select_n.59), kind=kOutput, calls=%fused_computation.59 | convolution fusion | flops 2684354560 | bytes 9437188 | tf_op jit(solution)/shard_map/pmk,pnk->mn/dot_general | solution.py:145
  285.1 0.4 copy-done.14
  285.5 4.0 bitcast_convert_fusion.4
  289.4 2.0 collective-permute-start.5
  291.4 7.6 %fusion.53.refs_1_ = f32[640,1024]{1,0:T(8,128)} fusion(bf16[4,640,512]{2,1,0:T(8,128)(2,1)} %copy-done.7, bf16[4,2048,512]{2,1,0:T(8,128)(2,1)} %all-gather.11.cloned.1.call-done, s32[]{:T(128)S(6)} %select_n.59), kind=kOutput, calls=%fused_computation.60 | convolution fusion | flops 2684354560 | bytes 9437188 | tf_op jit(solution)/shard_map/pmk,pnk->mn/dot_general | solution.py:145
  299.0 3.9 bitcast_convert_fusion.3
  303.0 43.7 %all-gather.13.cloned.1.call-done = bf16[4,2048,512]{2,1,0:T(8,128)(2,1)} async-done(((bf16[4,128,512]{2,1,0:T(8,128)(2,1)}), bf16[4,2048,512]{2,1,0:T(8,128)(2,1)}) %all-gather.13.cloned.1.call-update) | async-done | bytes 8388624 | tf_op jit(solution)/shard_map/all_gather | solution.py:139
  346.7 7.6 %fusion.56.refs_2_ = f32[640,1024]{1,0:T(8,128)} fusion(bf16[4,640,512]{2,1,0:T(8,128)(2,1)} %copy-done.7, bf16[4,2048,512]{2,1,0:T(8,128)(2,1)} %all-gather.13.cloned.1.call-done, s32[]{:T(128)S(6)} %select_n.59), kind=kOutput, calls=%fused_computation.61 | convolution fusion | flops 2684354560 | bytes 9437188 | tf_op jit(solution)/shard_map/pmk,pnk->mn/dot_general | solution.py:145
  354.3 4.0 bitcast_convert_fusion.2
  358.3 1.5 collective-permute-start.7
  359.7 62.2 %all-gather.15.cloned.1.call-done = bf16[4,2048,512]{2,1,0:T(8,128)(2,1)} async-done(((bf16[4,128,512]{2,1,0:T(8,128)(2,1)}), bf16[4,2048,512]{2,1,0:T(8,128)(2,1)}) %all-gather.15.cloned.1.call-update) | async-done | bytes 8388624 | tf_op jit(solution)/shard_map/all_gather | solution.py:139
  421.9 7.5 %fusion.59.refs_3_ = f32[640,1024]{1,0:T(8,128)} fusion(bf16[4,640,512]{2,1,0:T(8,128)(2,1)} %copy-done.7, bf16[4,2048,512]{2,1,0:T(8,128)(2,1)} %all-gather.15.cloned.1.call-done, s32[]{:T(128)S(6)} %select_n.59), kind=kOutput, calls=%fused_computation.62 | convolution fusion | flops 2684354560 | bytes 9437188 | tf_op jit(solution)/shard_map/pmk,pnk->mn/dot_general | solution.py:145
  429.4 4.0 bitcast_convert_fusion.1
  433.4 1.5 collective-permute-start.8
  434.9 62.3 %all-gather.17.cloned.1.call-done = bf16[4,2048,512]{2,1,0:T(8,128)(2,1)} async-done(((bf16[4,128,512]{2,1,0:T(8,128)(2,1)}), bf16[4,2048,512]{2,1,0:T(8,128)(2,1)}) %all-gather.17.cloned.1.call-update) | async-done | bytes 8388624 | tf_op jit(solution)/shard_map/all_gather | solution.py:139
  497.2 6.2 %bitcast_convert_fusion = bf16[640,1024]{1,0:T(8,128)(2,1)S(1)} fusion(bf16[4,640,512]{2,1,0:T(8,128)(2,1)} %copy-done.7, bf16[4,2048,512]{2,1,0:T(8,128)(2,1)} %all-gather.17.cloned.1.call-done, s32[]{:T(128)S(6)} %select_n.60), kind=kOutput, calls=%fused_computation.54 | convolution fusion | flops 2685009920 | bytes 8126468 | tf_op jit(solution)/shard_map/pmk,pnk->mn/dot_general | solution.py:145
  503.5 1.5 collective-permute-start.9
  505.0 2.9 fusion.62.refs_4_
  507.9 26.5 %collective-permute-done.9.refs_9_ = bf16[640,1024]{1,0:T(8,128)(2,1)S(1)} collective-permute-done((bf16[640,1024]{1,0:T(8,128)(2,1)S(1)}, bf16[640,1024]{1,0:T(8,128)(2,1)S(1)}, u32[]{:S(2)}, u32[]{:S(2)}) %collective-permute-start.9) | collective-permute-done | bytes 1310752 | tf_op jit(solution)/shard_map/ppermute | solution.py:152
  534.5 9.8 %shard_map.60 = f32[640,5120]{1,0:T(8,128)} custom-call(f32[640,1024]{1,0:T(8,128)S(1)} %fusion.50.refs_0_, f32[640,1024]{1,0:T(8,128)S(1)} %copy-done.4, f32[640,1024]{1,0:T(8,128)S(1)} %copy-done.5, f32[640,1024]{1,0:T(8,128)S(1)} %copy-done.6, f32[640,1024]{1,0:T(8,128)S(1)} %fusion.62.refs_4_, bf16[640,1024]{1,0:T(8,128)(2,1)} %collective-permute-done.5.refs_5_, ...), custom_call_target="tpu_custom_call" | custom-call | tf_op jit(solution)/shard_map/pallas_call | solution.py:89
  (53 shorter events, 0.4 us)
Async XLA Ops:
  6.5 3.6 copy-start
  6.5 93.7 %all-gather.7.cloned.1.call-start = ((), (), s32[]{:S(2)}) async-start(), calls=%async_computation | async-start | bytes 11141120 | tf_op jit(solution)/shard_map/all_gather | solution.py:109
  7.3 270.3 %all-gather.9.cloned.1.call-start = ((), (), s32[]{:S(2)}) async-start(), calls=%async_computation.1 | async-start | bytes 8912896 | tf_op jit(solution)/shard_map/all_gather | solution.py:139
  29.9 2.4 copy-start.2
  100.3 8.6 %copy-start.3 = (bf16[4,128,5120]{2,1,0:T(8,128)(2,1)S(1)}, bf16[4,128,5120]{2,1,0:T(8,128)(2,1)}, u32[]{:S(2)}) copy-start(bf16[4,128,5120]{2,1,0:T(8,128)(2,1)} %copy-done.2) | copy-start | bytes 15728644
  100.3 8.6 %copy-start.13 = (bf16[5120,1024]{0,1:T(8,128)(2,1)S(1)}, bf16[5120,1024]{0,1:T(8,128)(2,1)}, u32[]{:S(2)}) copy-start(bf16[5120,1024]{0,1:T(8,128)(2,1)} %all-gather.7.cloned.1.call-done) | copy-start | bytes 31457284
  107.4 14.2 %collective-permute-start = (bf16[4,128,512]{2,1,0:T(8,128)(2,1)S(1)}, bf16[4,128,512]{2,1,0:T(8,128)(2,1)S(1)}, u32[]{:S(2)}, u32[]{:S(2)}) collective-permute-start(bf16[4,128,512]{2,1,0:T(8,128)(2,1)S(1)} %fusion.75), channel_id=1, source_target_pairs={{0,1},{1,0},{2,3},{3,2},{4,5},{5,4},{6,7},{7,6},{8,9},{9,8},{10,11... | collective-permute-start | bytes 1572872 | tf_op jit(solution)/shard_map/ppermute | solution.py:132
  122.5 168.9 %all-gather.11.cloned.1.call-start = ((), (), s32[]{:S(2)}) async-start(), calls=%async_computation.2 | async-start | bytes 8912896 | tf_op jit(solution)/shard_map/all_gather | solution.py:139
  146.9 13.9 %collective-permute-start.1 = (bf16[4,128,512]{2,1,0:T(8,128)(2,1)S(1)}, bf16[4,128,512]{2,1,0:T(8,128)(2,1)S(1)}, u32[]{:S(2)}, u32[]{:S(2)}) collective-permute-start(bf16[4,128,512]{2,1,0:T(8,128)(2,1)S(1)} %fusion.78), channel_id=1, source_target_pairs={{0,1},{1,0},{2,3},{3,2},{4,5},{5,4},{6,7},{7,6},{8,9},{9,8},{10,11... | collective-permute-start | bytes 1572872 | tf_op jit(solution)/shard_map/ppermute | solution.py:132
  161.7 184.9 %all-gather.13.cloned.1.call-start = ((), (), s32[]{:S(2)}) async-start(), calls=%async_computation.3 | async-start | bytes 8912896 | tf_op jit(solution)/shard_map/all_gather | solution.py:139
  187.1 14.1 %collective-permute-start.2 = (bf16[4,128,512]{2,1,0:T(8,128)(2,1)S(1)}, bf16[4,128,512]{2,1,0:T(8,128)(2,1)S(1)}, u32[]{:S(2)}, u32[]{:S(2)}) collective-permute-start(bf16[4,128,512]{2,1,0:T(8,128)(2,1)S(1)} %fusion.81), channel_id=1, source_target_pairs={{0,1},{1,0},{2,3},{3,2},{4,5},{5,4},{6,7},{7,6},{8,9},{9,8},{10,11... | collective-permute-start | bytes 1572872 | tf_op jit(solution)/shard_map/ppermute | solution.py:132
  202.2 219.7 %all-gather.15.cloned.1.call-start = ((), (), s32[]{:S(2)}) async-start(), calls=%async_computation.4 | async-start | bytes 8912896 | tf_op jit(solution)/shard_map/all_gather | solution.py:139
  226.5 12.8 %collective-permute-start.3 = (bf16[4,128,512]{2,1,0:T(8,128)(2,1)S(1)}, bf16[4,128,512]{2,1,0:T(8,128)(2,1)S(1)}, u32[]{:S(2)}, u32[]{:S(2)}) collective-permute-start(bf16[4,128,512]{2,1,0:T(8,128)(2,1)S(1)} %fusion.84), channel_id=1, source_target_pairs={{0,1},{1,0},{2,3},{3,2},{4,5},{5,4},{6,7},{7,6},{8,9},{9,8},{10,11... | collective-permute-start | bytes 1572872 | tf_op jit(solution)/shard_map/ppermute | solution.py:132
  240.3 256.9 %all-gather.17.cloned.1.call-start = ((), (), s32[]{:S(2)}) async-start(), calls=%async_computation.5 | async-start | bytes 8912896 | tf_op jit(solution)/shard_map/all_gather | solution.py:139
  266.6 10.0 %collective-permute-start.4 = (bf16[4,128,512]{2,1,0:T(8,128)(2,1)S(1)}, bf16[4,128,512]{2,1,0:T(8,128)(2,1)S(1)}, u32[]{:S(2)}, u32[]{:S(2)}) collective-permute-start(bf16[4,128,512]{2,1,0:T(8,128)(2,1)S(1)} %fusion.87), channel_id=1, source_target_pairs={{0,1},{1,0},{2,3},{3,2},{4,5},{5,4},{6,7},{7,6},{8,9},{9,8},{10,11... | collective-permute-start | bytes 1572872 | tf_op jit(solution)/shard_map/ppermute | solution.py:132
  277.5 1.5 copy-start.7
  279.0 6.1 %copy-start.8 = (bf16[4,640,512]{2,1,0:T(8,128)(2,1)S(1)}, bf16[4,640,512]{2,1,0:T(8,128)(2,1)}, u32[]{:S(2)}) copy-start(bf16[4,640,512]{2,1,0:T(8,128)(2,1)} %copy-done.7) | copy-start | bytes 7864324
  279.0 6.5 %copy-start.14 = (bf16[4,2048,512]{2,1,0:T(8,128)(2,1)S(1)}, bf16[4,2048,512]{2,1,0:T(8,128)(2,1)}, u32[]{:S(2)}) copy-start(bf16[4,2048,512]{2,1,0:T(8,128)(2,1)} %all-gather.9.cloned.1.call-done) | copy-start | bytes 25165828
  289.4 218.4 %collective-permute-start.5 = (bf16[640,1024]{1,0:T(8,128)(2,1)}, bf16[640,1024]{1,0:T(8,128)(2,1)}, u32[]{:S(2)}, u32[]{:S(2)}) collective-permute-start(bf16[640,1024]{1,0:T(8,128)(2,1)} %bitcast_convert_fusion.4), channel_id=1, source_target_pairs={{0,1},{1,0},{2,3},{3,2},{4,5},{5,4},{6,7},{7,6},{8,9},{9,8},{10,11... | collective-permute-start | bytes 3932168 | tf_op jit(solution)/shard_map/ppermute | solution.py:152
  291.4 7.6 %copy-start.9 = (bf16[4,640,512]{2,1,0:T(8,128)(2,1)S(1)}, bf16[4,640,512]{2,1,0:T(8,128)(2,1)}, u32[]{:S(2)}) copy-start(bf16[4,640,512]{2,1,0:T(8,128)(2,1)} %copy-done.7) | copy-start | bytes 7864324
  291.4 7.6 %copy-start.15 = (bf16[4,2048,512]{2,1,0:T(8,128)(2,1)S(1)}, bf16[4,2048,512]{2,1,0:T(8,128)(2,1)}, u32[]{:S(2)}) copy-start(bf16[4,2048,512]{2,1,0:T(8,128)(2,1)} %all-gather.11.cloned.1.call-done) | copy-start | bytes 25165828
  303.0 204.9 %collective-permute-start.6 = (bf16[640,1024]{1,0:T(8,128)(2,1)}, bf16[640,1024]{1,0:T(8,128)(2,1)}, u32[]{:S(2)}, u32[]{:S(2)}) collective-permute-start(bf16[640,1024]{1,0:T(8,128)(2,1)} %bitcast_convert_fusion.3), channel_id=1, source_target_pairs={{0,1},{1,0},{2,3},{3,2},{4,5},{5,4},{6,7},{7,6},{8,9},{9,8},{10,11... | collective-permute-start | bytes 3932168 | tf_op jit(solution)/shard_map/ppermute | solution.py:152
  346.7 7.6 %copy-start.10 = (bf16[4,640,512]{2,1,0:T(8,128)(2,1)S(1)}, bf16[4,640,512]{2,1,0:T(8,128)(2,1)}, u32[]{:S(2)}) copy-start(bf16[4,640,512]{2,1,0:T(8,128)(2,1)} %copy-done.7) | copy-start | bytes 7864324
  346.7 7.6 %copy-start.16 = (bf16[4,2048,512]{2,1,0:T(8,128)(2,1)S(1)}, bf16[4,2048,512]{2,1,0:T(8,128)(2,1)}, u32[]{:S(2)}) copy-start(bf16[4,2048,512]{2,1,0:T(8,128)(2,1)} %all-gather.13.cloned.1.call-done) | copy-start | bytes 25165828
  358.3 149.6 %collective-permute-start.7 = (bf16[640,1024]{1,0:T(8,128)(2,1)}, bf16[640,1024]{1,0:T(8,128)(2,1)}, u32[]{:S(2)}, u32[]{:S(2)}) collective-permute-start(bf16[640,1024]{1,0:T(8,128)(2,1)} %bitcast_convert_fusion.2), channel_id=1, source_target_pairs={{0,1},{1,0},{2,3},{3,2},{4,5},{5,4},{6,7},{7,6},{8,9},{9,8},{10,11... | collective-permute-start | bytes 3932168 | tf_op jit(solution)/shard_map/ppermute | solution.py:152
  421.9 7.5 %copy-start.11 = (bf16[4,640,512]{2,1,0:T(8,128)(2,1)S(1)}, bf16[4,640,512]{2,1,0:T(8,128)(2,1)}, u32[]{:S(2)}) copy-start(bf16[4,640,512]{2,1,0:T(8,128)(2,1)} %copy-done.7) | copy-start | bytes 7864324
  421.9 7.5 %copy-start.17 = (bf16[4,2048,512]{2,1,0:T(8,128)(2,1)S(1)}, bf16[4,2048,512]{2,1,0:T(8,128)(2,1)}, u32[]{:S(2)}) copy-start(bf16[4,2048,512]{2,1,0:T(8,128)(2,1)} %all-gather.15.cloned.1.call-done) | copy-start | bytes 25165828
  433.4 74.5 %collective-permute-start.8 = (bf16[640,1024]{1,0:T(8,128)(2,1)}, bf16[640,1024]{1,0:T(8,128)(2,1)}, u32[]{:S(2)}, u32[]{:S(2)}) collective-permute-start(bf16[640,1024]{1,0:T(8,128)(2,1)} %bitcast_convert_fusion.1), channel_id=1, source_target_pairs={{0,1},{1,0},{2,3},{3,2},{4,5},{5,4},{6,7},{7,6},{8,9},{9,8},{10,11... | collective-permute-start | bytes 3932168 | tf_op jit(solution)/shard_map/ppermute | solution.py:152
  497.2 7.8 %copy-start.12 = (bf16[4,640,512]{2,1,0:T(8,128)(2,1)S(1)}, bf16[4,640,512]{2,1,0:T(8,128)(2,1)}, u32[]{:S(2)}) copy-start(bf16[4,640,512]{2,1,0:T(8,128)(2,1)} %copy-done.7) | copy-start | bytes 7864324
  497.2 7.8 %copy-start.18 = (bf16[4,2048,512]{2,1,0:T(8,128)(2,1)S(1)}, bf16[4,2048,512]{2,1,0:T(8,128)(2,1)}, u32[]{:S(2)}) copy-start(bf16[4,2048,512]{2,1,0:T(8,128)(2,1)} %all-gather.17.cloned.1.call-done) | copy-start | bytes 25165828
  503.4 31.0 %copy-start.4 = (f32[640,1024]{1,0:T(8,128)S(1)}, f32[640,1024]{1,0:T(8,128)}, u32[]{:S(2)}) copy-start(f32[640,1024]{1,0:T(8,128)} %fusion.53.refs_1_) | copy-start | bytes 7864324
  503.4 31.0 %copy-start.5 = (f32[640,1024]{1,0:T(8,128)S(1)}, f32[640,1024]{1,0:T(8,128)}, u32[]{:S(2)}) copy-start(f32[640,1024]{1,0:T(8,128)} %fusion.56.refs_2_) | copy-start | bytes 7864324
  503.4 31.0 %copy-start.6 = (f32[640,1024]{1,0:T(8,128)S(1)}, f32[640,1024]{1,0:T(8,128)}, u32[]{:S(2)}) copy-start(f32[640,1024]{1,0:T(8,128)} %fusion.59.refs_3_) | copy-start | bytes 7864324
  503.5 31.0 %collective-permute-start.9 = (bf16[640,1024]{1,0:T(8,128)(2,1)S(1)}, bf16[640,1024]{1,0:T(8,128)(2,1)S(1)}, u32[]{:S(2)}, u32[]{:S(2)}) collective-permute-start(bf16[640,1024]{1,0:T(8,128)(2,1)S(1)} %bitcast_convert_fusion), channel_id=1, source_target_pairs={{0,1},{1,0},{2,3},{3,2},{4,5},{5,4},{6,7},{7,6},{8,9},{9,8},{10,11... | collective-permute-start | bytes 3932168 | tf_op jit(solution)/shard_map/ppermute | solution.py:152
  534.5 9.8 %copy-start.1 = (s32[80,80]{1,0:T(8,128)S(1)}, s32[80,80]{1,0:T(8,128)}, u32[]{:S(2)}) copy-start(s32[80,80]{1,0:T(8,128)} %param.8) | copy-start | bytes 76804
Sparse Core Ops, SparseCore 0:
  9.6 90.5 all-gather.6
  122.7 73.1 all-gather.8
  198.0 73.1 all-gather.10
  273.3 73.3 all-gather.12
  348.7 73.1 all-gather.14
  424.0 73.1 all-gather.16

commit v2 on v1

--- a/solution.py
+++ b/solution.py
@@ -11,7 +11,8 @@
 NOCC = 1024
 BLK = 128
 AUX = 4
-CHUNKS = 5
+PIECES = (3, 2)
+CHUNKS = len(PIECES)
 SUB = 64
 
 
@@ -47,9 +48,9 @@
                 out_ref[p, :, cols] = (pre * (weight * value)).astype(out_ref.dtype)
 
 
-def tile_chunk(pair_prefactor, boys_argument, order, screen, chunk, height):
+def tile_chunk(pair_prefactor, boys_argument, order, screen, start, height):
     aux, _, width = pair_prefactor.shape
-    first = chunk * height // SUB
+    first = start // SUB
     wide = width // 2
     spec = pl.BlockSpec((aux, SUB, wide), lambda i, j, *_: (0, first + i, j))
     return pl.pallas_call(
@@ -70,7 +71,7 @@
     )(order, screen, pair_prefactor, boys_argument)
 
 
-def assemble_kernel(height, per, scale, *refs):
+def assemble_kernel(heights, starts, per, scale, *refs):
     own, received, out_ref = refs[:CHUNKS], refs[CHUNKS:-1], refs[-1]
     extra = len(received) // CHUNKS
     for chunk in range(CHUNKS):
@@ -79,19 +80,21 @@
             total = total + part[...].astype(jnp.float32)
         total = total * scale
         for s in range(per):
-            at = s * CHUNKS * height + chunk * height
+            height = heights[chunk]
+            at = s * sum(heights) + starts[chunk]
             out_ref[:, at : at + height] = total[:, s * height : (s + 1) * height]
 
 
-def assemble(own, received, height, per, scale):
-    rows, span = own[0].shape
-    spec = pl.BlockSpec((SUB, span), lambda i: (i, 0))
+def assemble(own, received, heights, starts, per, scale):
+    rows = own[0].shape[0]
+    width = per * sum(heights)
+    spec = lambda a: pl.BlockSpec((SUB, a.shape[1]), lambda i: (i, 0))
     return pl.pallas_call(
-        functools.partial(assemble_kernel, height, per, scale),
-        out_shape=jax.ShapeDtypeStruct((rows, CHUNKS * span), jnp.float32),
+        functools.partial(assemble_kernel, heights, starts, per, scale),
+        out_shape=jax.ShapeDtypeStruct((rows, width), jnp.float32),
         grid=(rows // SUB,),
-        in_specs=[spec] * (len(own) + len(received)),
-        out_specs=pl.BlockSpec((SUB, CHUNKS * span), lambda i: (i, 0)),
+        in_specs=[spec(a) for a in own + received],
+        out_specs=pl.BlockSpec((SUB, width), lambda i: (i, 0)),
         compiler_params=pltpu.CompilerParams(vmem_limit_bytes=32 << 20),
     )(*own, *received)
 
@@ -100,10 +103,10 @@
     mine_rows, mine_cols = pair_prefactor.shape[1:]
     row_index = lax.axis_index("row")
     col_index = lax.axis_index("col")
-    height = mine_rows // CHUNKS
+    heights = [mine_rows * piece // sum(PIECES) for piece in PIECES]
+    starts = [sum(heights[:i]) for i in range(CHUNKS)]
     share = NOCC // cols
     per = mine_cols // mine_rows
-    span = per * height
     scale = 1.0 / math.sqrt(AUX * NOCC)
 
     coeff_all = lax.all_gather(orbitals, "row", axis=1, tiled=True)
@@ -124,7 +127,7 @@
     for chunk in range(CHUNKS):
         if chunk >= 2:
             order = lax.optimization_barrier((order, shares[chunk - 2]))[0]
-        tiles.append(tile_chunk(pair_prefactor, boys_argument, order, screen, chunk, height))
+        tiles.append(tile_chunk(pair_prefactor, boys_argument, order, screen, starts[chunk], heights[chunk]))
         tile = tiles[-1]
         if chunk >= 1:
             tile = lax.optimization_barrier((tile, shares[chunk - 1]))[0]
@@ -135,14 +138,16 @@
         total = lax.optimization_barrier(project(tile, coeff[0]))
         for part in received:
             total = total + part.astype(jnp.float32)
-        shares.append(total.astype(jnp.bfloat16))
-        panels.append(lax.all_gather(shares[-1], "row", axis=1, tiled=True))
+        total = total.astype(jnp.bfloat16)
+        shares.append(jnp.concatenate([total[p] for p in range(AUX)], axis=1))
+        panels.append(lax.all_gather(shares[-1], "row", axis=0, tiled=True))
 
-    mine = jnp.concatenate(shares, axis=1)
+    mine = jnp.concatenate(shares, axis=0)
 
     def product(panel, peer):
-        other = lax.dynamic_slice_in_dim(panel, peer * span, span, 1)
-        return jnp.einsum("pmk,pnk->mn", mine, other, preferred_element_type=jnp.float32)
+        span = panel.shape[0] // cols
+        other = lax.dynamic_slice_in_dim(panel, peer * span, span, 0)
+        return jnp.einsum("mk,nk->mn", mine, other, preferred_element_type=jnp.float32)
 
     own, received = [], []
     for chunk, panel in enumerate(panels):
@@ -153,7 +158,7 @@
             for k in range(1, cols)
         ]
         own.append(lax.optimization_barrier(product(panel, peers[0])))
-    return assemble(own, received, height, per, scale)
+    return assemble(own, received, heights, starts, per, scale)
 
 
 def solution(mesh):

time: 559 us -> 521 us (0.932)
  waiting for transfers between devices: 299 us -> 236 us
  matrix products: 105 us -> 135 us
  starting transfers between devices: 14.6 us -> 4.66 us
    all_gather x5 -> x2, waiting for transfers between devices: 168 us -> 123 us  [body(): panels.append(lax.all_gather(shares[-1], 'row', axis=0, tiled=True))]
    all_gather x1, waiting for transfers between devices: 68 us -> 23.9 us  [body(): coeff_all = lax.all_gather(orbitals, 'row', axis=1, tiled=True)]
    dot_general x10 -> x4, matrix products: 53.8 us -> 92.2 us  [product(): jnp.einsum('mk,nk->mn', mine, other, preferred_element_type=jnp.float32)]
    ppermute x5 -> x2, waiting for transfers between devices: 26.5 us -> 48.2 us  [body(): lax.ppermute(product(panel, peers[k]).astype(jnp.bfloat16), 'col', paths[k])]
    dot_general x10 -> x4, matrix products: 51.7 us -> 43.2 us  [project(): jnp.einsum('pmn,nk->pmk', tile, part, preferred_element_type=jnp.float32)]
    ppermute x5 -> x2, waiting for transfers between devices: 35.4 us -> 40.1 us  [body(): lax.ppermute(project(tile, coeff[k]).astype(jnp.bfloat16), 'col', paths[k])]
    pallas_call x5 -> x2, Pallas kernels: 95.4 us -> 97.1 us  [tile_chunk(): pl.pallas_call(functools.partial(tile_kernel, first), out_shape=jax.Shape...]
  transfers between devices with their start and end apart: 16 -> 7, of which waited for: 10 -> 6; matrix products, arithmetic and copies ran while one was open for 19% -> 25% of each run, Pallas kernels for 17% -> 19%
where the time goes in v2:
time: 521 us; the launch traced here: 514 us
  waiting for transfers between devices  236 us (45%)
  matrix products  135 us (26%)
  Pallas kernels  106 us (20%)
  between operations  13.6 us (3%)
  local copies, waits for them, and re-layouts  13 us (2%)
    all_gather x2, waiting for transfers between devices, body(): panels.append(lax.all_gather(shares[-1], 'row', axis=0, tiled=True))  123 us
    pallas_call x2, Pallas kernels, tile_chunk(): pl.pallas_call(functools.partial(tile_kernel, first), out_shape=jax.Shape...  97.1 us
    dot_general x4, matrix products, product(): jnp.einsum('mk,nk->mn', mine, other, preferred_element_type=jnp.float32)  92.2 us
    ppermute x2, waiting for transfers between devices, body(): lax.ppermute(product(panel, peers[k]).astype(jnp.bfloat16), 'col', paths[k])  48.2 us
    dot_general x4, matrix products, project(): jnp.einsum('pmn,nk->pmk', tile, part, preferred_element_type=jnp.float32)  43.2 us
    ppermute x2, waiting for transfers between devices, body(): lax.ppermute(project(tile, coeff[k]).astype(jnp.bfloat16), 'col', paths[k])  40.1 us
    all_gather x1, waiting for transfers between devices, body(): coeff_all = lax.all_gather(orbitals, 'row', axis=1, tiled=True)  23.9 us
  transfers between devices with their start and end apart: 7, of which 6 were waited for; matrix products, arithmetic and copies ran while one was open for 25% of the time, Pallas kernels for 19%

profile of v2, /device:TPU:0, one launch (start us, length us, event | category | flops | bytes accessed | tf_op | source)
XLA Modules:
  0.0 514.3 jit_solution(14688000930355395976)
XLA Ops:
  6.5 0.0 copy-start
  6.5 0.0 all-gather.4.cloned.1.call-start
  6.5 0.7 all-gather.4.cloned.1.call-update
  7.3 0.0 all-gather.6.cloned.1.call-start
  7.3 1.4 gather_fusion.1
  8.8 1.3 gather_fusion
  10.1 0.0 copy-done
  10.1 0.6 gather_fusion.2
  10.7 0.1 copy.12
  10.8 0.6 gather_fusion.3
  11.4 0.1 copy.13
  11.5 0.1 broadcast_add_fusion.order_ref
  11.5 59.5 %shard_map.55 = bf16[4,384,5120]{2,1,0:T(8,128)(2,1)S(1)} custom-call(s32[10,40]{1,0:T(8,128)S(1)} %broadcast_add_fusion.order_ref, s32[10,40]{1,0:T(8,128)S(1)} %bitcast.43, bf16[4,640,5120]{2,1,0:T(8,128)(2,1)} %pre_ref.3, bf16[4,640,5120]{2,1,0:T(8,128)(2,1)} %arg_ref.3), custom_call_target="tpu_custom_call" | custom-call | flops 471859200 | bytes 47185920 | tf_op jit(solution)/shard_map/pallas_call | solution.py:56
  71.1 0.0 copy-start.2
  71.1 5.5 %copy-done.2 = bf16[4,384,5120]{2,1,0:T(8,128)(2,1)} copy-done((bf16[4,384,5120]{2,1,0:T(8,128)(2,1)}, bf16[4,384,5120]{2,1,0:T(8,128)(2,1)S(1)}, u32[]{:S(2)}) %copy-start.2) | copy-done | bytes 15728664
  76.5 23.9 %all-gather.4.cloned.1.call-done = bf16[5120,1024]{0,1:T(8,128)(2,1)} async-done(((bf16[5120,64]{0,1:T(8,128)(2,1)}), bf16[5120,1024]{0,1:T(8,128)(2,1)}) %all-gather.4.cloned.1.call-update) | async-done | bytes 10485776 | tf_op jit(solution)/shard_map/all_gather | solution.py:112
  100.5 0.0 copy-start.3
  100.5 14.3 %fusion.26 = bf16[4,384,512]{2,1,0:T(8,128)(2,1)} fusion(bf16[4,384,5120]{2,1,0:T(8,128)(2,1)} %copy-done.2, bf16[5120,1024]{0,1:T(8,128)(2,1)} %all-gather.4.cloned.1.call-done, s32[]{:T(128)S(6)} %select_n.56), kind=kOutput, calls=%fused_computation.29 | convolution fusion | flops 8053850112 | bytes 22544388 | tf_op jit(solution)/shard_map/pmn,nk->pmk/dot_general | solution.py:124
  114.7 1.5 collective-permute-start
  116.2 0.0 copy-done.3
  116.2 13.3 %fusion.14 = f32[4,384,512]{2,1,0:T(8,128)S(1)} fusion(bf16[4,384,5120]{2,1,0:T(8,128)(2,1)S(1)} %copy-done.3, bf16[5120,1024]{0,1:T(8,128)(2,1)} %all-gather.4.cloned.1.call-done, s32[]{:T(128)S(6)} %select_n.55), kind=kOutput, calls=%fused_computation.18 | convolution fusion | flops 8053063680 | bytes 24117252 | tf_op jit(solution)/shard_map/pmn,nk->pmk/dot_general | solution.py:124
  129.5 22.1 %collective-permute-done = bf16[4,384,512]{2,1,0:T(8,128)(2,1)} collective-permute-done((bf16[4,384,512]{2,1,0:T(8,128)(2,1)}, bf16[4,384,512]{2,1,0:T(8,128)(2,1)}, u32[]{:S(2)}, u32[]{:S(2)}) %collective-permute-start) | collective-permute-done | bytes 1572896 | tf_op jit(solution)/shard_map/ppermute | solution.py:135
  151.6 1.9 add_convert_fusion
  153.5 0.1 slice_bitcast_fusion.3
  153.7 0.0 copy-start.5
  153.7 0.0 copy-start.6
  153.7 1.4 pad_maximum_fusion
  155.1 0.0 all-gather.6.cloned.1.call-update
  155.1 0.0 all-gather.8.cloned.1.call-start
  155.1 37.6 %shard_map.56 = bf16[4,256,5120]{2,1,0:T(8,128)(2,1)S(1)} custom-call(s32[10,40]{1,0:T(8,128)S(1)} %broadcast_add_fusion.order_ref, s32[10,40]{1,0:T(8,128)S(1)} %bitcast.44, bf16[4,640,5120]{2,1,0:T(8,128)(2,1)} %pre_ref.3, bf16[4,640,5120]{2,1,0:T(8,128)(2,1)} %arg_ref.3), custom_call_target="tpu_custom_call" | custom-call | flops 314572800 | bytes 31457280 | tf_op jit(solution)/shard_map/pallas_call | solution.py:56
  192.7 7.6 %fusion.29 = bf16[4,256,512]{2,1,0:T(8,128)(2,1)S(1)} fusion(bf16[4,256,5120]{2,1,0:T(8,128)(2,1)S(1)} %shard_map.56, bf16[5120,1024]{0,1:T(8,128)(2,1)} %all-gather.4.cloned.1.call-done, s32[]{:T(128)S(6)} %select_n.56), kind=kOutput, calls=%fused_computation.31 | convolution fusion | flops 5369233408 | bytes 16777220 | tf_op jit(solution)/shard_map/pmn,nk->pmk/dot_general | solution.py:124
  200.4 0.1 collective-permute-start.1
  200.5 8.0 %fusion.12 = f32[4,256,512]{2,1,0:T(8,128)S(1)} fusion(bf16[4,256,5120]{2,1,0:T(8,128)(2,1)S(1)} %shard_map.56, bf16[5120,1024]{0,1:T(8,128)(2,1)} %all-gather.4.cloned.1.call-done, s32[]{:T(128)S(6)} %select_n.55), kind=kOutput, calls=%fused_computation.16 | convolution fusion | flops 5368709120 | bytes 17825796 | tf_op jit(solution)/shard_map/pmn,nk->pmk/dot_general | solution.py:124
  208.5 18.0 %collective-permute-done.1 = bf16[4,256,512]{2,1,0:T(8,128)(2,1)S(1)} collective-permute-done((bf16[4,256,512]{2,1,0:T(8,128)(2,1)S(1)}, bf16[4,256,512]{2,1,0:T(8,128)(2,1)S(1)}, u32[]{:S(2)}, u32[]{:S(2)}) %collective-permute-start.1) | collective-permute-done | bytes 1048608 | tf_op jit(solution)/shard_map/ppermute | solution.py:135
  226.4 0.4 add_convert_fusion.1
  226.8 0.1 slice_bitcast_fusion.7
  226.9 0.0 copy-start.7
  226.9 0.0 copy-start.8
  226.9 0.0 copy-start.9
  226.9 0.0 copy-start.10
  226.9 1.3 pad_maximum_fusion.1
  228.2 0.0 all-gather.8.cloned.1.call-update
  228.2 53.7 %all-gather.6.cloned.1.call-done = bf16[6144,2048]{1,0:T(8,128)(2,1)} async-done(((bf16[384,2048]{1,0:T(8,128)(2,1)}), bf16[6144,2048]{1,0:T(8,128)(2,1)}) %all-gather.6.cloned.1.call-update) | async-done | bytes 25165840 | tf_op jit(solution)/shard_map/all_gather | solution.py:143
  282.0 28.7 %fusion.16 = bf16[640,3072]{1,0:T(8,128)(2,1)} fusion(bf16[6144,2048]{1,0:T(8,128)(2,1)} %all-gather.6.cloned.1.call-done, s32[]{:T(128)S(6)} %select_n.59, bf16[256,512]{1,0:T(8,128)(2,1)S(1)} %get-tuple-element.14, bf16[256,512]{1,0:T(8,128)(2,1)S(1)} %get-tuple-element.15, bf16[256,512]{1,0:T(8,128)(2,1)S(1)} %get-tuple-element.16, ...), kind=kOutput, calls=%fused_computation.20 | convolution fusion | flops 8076001280 | bytes 19136516 | tf_op jit(solution)/shard_map/mk,nk->mn/dot_general | solution.py:150
  310.7 1.5 collective-permute-start.2
  312.2 29.2 %fusion.2.refs_0_ = f32[640,3072]{1,0:T(8,128)} fusion(bf16[6144,2048]{1,0:T(8,128)(2,1)} %all-gather.6.cloned.1.call-done, s32[]{:T(128)S(6)} %select_n.57, bf16[256,512]{1,0:T(8,128)(2,1)S(1)} %get-tuple-element.14, bf16[256,512]{1,0:T(8,128)(2,1)S(1)} %get-tuple-element.15, bf16[256,512]{1,0:T(8,128)(2,1)S(1)} %get-tuple-element.16, ...), kind=kOutput, calls=%fused_computation.6 | convolution fusion | flops 8074035200 | bytes 23068676 | tf_op jit(solution)/shard_map/mk,nk->mn/dot_general | solution.py:150
  341.4 69.7 %all-gather.8.cloned.1.call-done = bf16[4096,2048]{1,0:T(8,128)(2,1)} async-done(((bf16[256,2048]{1,0:T(8,128)(2,1)}), bf16[4096,2048]{1,0:T(8,128)(2,1)}) %all-gather.8.cloned.1.call-update) | async-done | bytes 16777232 | tf_op jit(solution)/shard_map/all_gather | solution.py:143
  411.0 0.0 copy-done.5
  411.1 0.0 copy-done.6
  411.1 0.0 copy-done.7
  411.1 0.0 copy-done.8
  411.1 0.0 copy-done.9
  411.1 0.0 copy-done.10
  411.1 24.7 %fusion.23 = bf16[640,2048]{1,0:T(8,128)(2,1)} fusion(bf16[4096,2048]{1,0:T(8,128)(2,1)} %all-gather.8.cloned.1.call-done, s32[]{:T(128)S(6)} %select_n.60, bf16[256,512]{1,0:T(8,128)(2,1)S(1)} %get-tuple-element.14, bf16[256,512]{1,0:T(8,128)(2,1)S(1)} %get-tuple-element.15, bf16[256,512]{1,0:T(8,128)(2,1)S(1)} %get-tuple-element.16, ...), kind=kOutput, calls=%fused_computation.25 | convolution fusion | flops 5390991360 | bytes 13631492 | tf_op jit(solution)/shard_map/mk,nk->mn/dot_general | solution.py:150
  435.8 1.5 collective-permute-start.3
  437.3 9.6 %fusion.6.refs_1_ = f32[640,2048]{1,0:T(8,128)S(1)} fusion(bf16[4096,2048]{1,0:T(8,128)(2,1)} %all-gather.8.cloned.1.call-done, s32[]{:T(128)S(6)} %select_n.58, bf16[256,512]{1,0:T(8,128)(2,1)} %copy-done.8, bf16[256,512]{1,0:T(8,128)(2,1)} %copy-done.9, bf16[256,512]{1,0:T(8,128)(2,1)} %copy-done.10, bf16[256,512]{1,0:T(8,128)(2,1)} %copy-done.7, ...), kind=kOutput, calls=%fused_computation.10 | convolution fusion | flops 5389680640 | bytes 16252932 | tf_op jit(solution)/shard_map/mk,nk->mn/dot_general | solution.py:150
  446.9 48.2 %collective-permute-done.3.refs_3_ = bf16[640,2048]{1,0:T(8,128)(2,1)S(1)} collective-permute-done((bf16[640,2048]{1,0:T(8,128)(2,1)}, bf16[640,2048]{1,0:T(8,128)(2,1)S(1)}, u32[]{:S(2)}, u32[]{:S(2)}) %collective-permute-start.3) | collective-permute-done | bytes 2621472 | tf_op jit(solution)/shard_map/ppermute | solution.py:157
  495.1 0.0 collective-permute-done.2.refs_2_
  495.1 0.0 copy-start.4
  495.1 3.2 copy-done.4
  498.3 0.0 copy-start.1
  498.3 9.2 %shard_map.57 = f32[640,5120]{1,0:T(8,128)} custom-call(f32[640,3072]{1,0:T(8,128)S(1)} %copy-done.4, f32[640,2048]{1,0:T(8,128)S(1)} %fusion.6.refs_1_, bf16[640,3072]{1,0:T(8,128)(2,1)} %collective-permute-done.2.refs_2_, bf16[640,2048]{1,0:T(8,128)(2,1)S(1)} %collective-permute-done.3.refs_3_), custom_call_target="tpu_custom_call" | custom-call | tf_op jit(solution)/shard_map/pallas_call | solution.py:92
  507.5 0.0 copy-done.1
  (4 shorter events, 0.0 us)
Async XLA Ops:
  6.5 3.6 copy-start
  6.5 93.9 %all-gather.4.cloned.1.call-start = ((), (), s32[]{:S(2)}) async-start(), calls=%async_computation | async-start | bytes 11141120 | tf_op jit(solution)/shard_map/all_gather | solution.py:112
  7.3 274.7 %all-gather.6.cloned.1.call-start = ((), (), s32[]{:S(2)}) async-start(), calls=%async_computation.1 | async-start | bytes 26738688 | tf_op jit(solution)/shard_map/all_gather | solution.py:143
  71.1 5.5 %copy-start.2 = (bf16[4,384,5120]{2,1,0:T(8,128)(2,1)}, bf16[4,384,5120]{2,1,0:T(8,128)(2,1)S(1)}, u32[]{:S(2)}) copy-start(bf16[4,384,5120]{2,1,0:T(8,128)(2,1)S(1)} %shard_map.55) | copy-start | bytes 47185924
  100.5 15.7 %copy-start.3 = (bf16[4,384,5120]{2,1,0:T(8,128)(2,1)S(1)}, bf16[4,384,5120]{2,1,0:T(8,128)(2,1)}, u32[]{:S(2)}) copy-start(bf16[4,384,5120]{2,1,0:T(8,128)(2,1)} %copy-done.2) | copy-start | bytes 47185924
  114.7 36.9 %collective-permute-start = (bf16[4,384,512]{2,1,0:T(8,128)(2,1)}, bf16[4,384,512]{2,1,0:T(8,128)(2,1)}, u32[]{:S(2)}, u32[]{:S(2)}) collective-permute-start(bf16[4,384,512]{2,1,0:T(8,128)(2,1)} %fusion.26), channel_id=1, source_target_pairs={{0,1},{1,0},{2,3},{3,2},{4,5},{5,4},{6,7},{7,6},{8,9},{9,8},{10,11... | collective-permute-start | bytes 4718600 | tf_op jit(solution)/shard_map/ppermute | solution.py:135
  153.7 257.4 %copy-start.5 = (bf16[384,512]{1,0:T(8,128)(2,1)}, bf16[384,512]{1,0:T(8,128)(2,1)S(1)}, u32[]{:S(2)}) copy-start(bf16[384,512]{1,0:T(8,128)(2,1)S(1)} %get-tuple-element.11) | copy-start | bytes 1179652
  153.7 257.4 %copy-start.6 = (bf16[384,512]{1,0:T(8,128)(2,1)}, bf16[384,512]{1,0:T(8,128)(2,1)S(1)}, u32[]{:S(2)}) copy-start(bf16[384,512]{1,0:T(8,128)(2,1)S(1)} %get-tuple-element.12) | copy-start | bytes 1179652
  155.1 256.0 %all-gather.8.cloned.1.call-start = ((), (), s32[]{:S(2)}) async-start(), calls=%async_computation.2 | async-start | bytes 17825792 | tf_op jit(solution)/shard_map/all_gather | solution.py:143
  200.4 26.0 %collective-permute-start.1 = (bf16[4,256,512]{2,1,0:T(8,128)(2,1)S(1)}, bf16[4,256,512]{2,1,0:T(8,128)(2,1)S(1)}, u32[]{:S(2)}, u32[]{:S(2)}) collective-permute-start(bf16[4,256,512]{2,1,0:T(8,128)(2,1)S(1)} %fusion.29), channel_id=1, source_target_pairs={{0,1},{1,0},{2,3},{3,2},{4,5},{5,4},{6,7},{7,6},{8,9},{9,8},{10,11... | collective-permute-start | bytes 3145736 | tf_op jit(solution)/shard_map/ppermute | solution.py:135
  226.9 184.2 %copy-start.7 = (bf16[256,512]{1,0:T(8,128)(2,1)}, bf16[256,512]{1,0:T(8,128)(2,1)S(1)}, u32[]{:S(2)}) copy-start(bf16[256,512]{1,0:T(8,128)(2,1)S(1)} %get-tuple-element.13) | copy-start | bytes 786436
  226.9 184.2 %copy-start.8 = (bf16[256,512]{1,0:T(8,128)(2,1)}, bf16[256,512]{1,0:T(8,128)(2,1)S(1)}, u32[]{:S(2)}) copy-start(bf16[256,512]{1,0:T(8,128)(2,1)S(1)} %get-tuple-element.14) | copy-start | bytes 786436
  226.9 184.2 %copy-start.9 = (bf16[256,512]{1,0:T(8,128)(2,1)}, bf16[256,512]{1,0:T(8,128)(2,1)S(1)}, u32[]{:S(2)}) copy-start(bf16[256,512]{1,0:T(8,128)(2,1)S(1)} %get-tuple-element.15) | copy-start | bytes 786436
  226.9 184.2 %copy-start.10 = (bf16[256,512]{1,0:T(8,128)(2,1)}, bf16[256,512]{1,0:T(8,128)(2,1)S(1)}, u32[]{:S(2)}) copy-start(bf16[256,512]{1,0:T(8,128)(2,1)S(1)} %get-tuple-element.16) | copy-start | bytes 786436
  310.7 184.4 %collective-permute-start.2 = (bf16[640,3072]{1,0:T(8,128)(2,1)}, bf16[640,3072]{1,0:T(8,128)(2,1)}, u32[]{:S(2)}, u32[]{:S(2)}) collective-permute-start(bf16[640,3072]{1,0:T(8,128)(2,1)} %fusion.16), channel_id=1, source_target_pairs={{0,1},{1,0},{2,3},{3,2},{4,5},{5,4},{6,7},{7,6},{8,9},{9,8},{10,11... | collective-permute-start | bytes 11796488 | tf_op jit(solution)/shard_map/ppermute | solution.py:157
  435.8 59.3 %collective-permute-start.3 = (bf16[640,2048]{1,0:T(8,128)(2,1)}, bf16[640,2048]{1,0:T(8,128)(2,1)S(1)}, u32[]{:S(2)}, u32[]{:S(2)}) collective-permute-start(bf16[640,2048]{1,0:T(8,128)(2,1)} %fusion.23), channel_id=1, source_target_pairs={{0,1},{1,0},{2,3},{3,2},{4,5},{5,4},{6,7},{7,6},{8,9},{9,8},{10,11... | collective-permute-start | bytes 7864328 | tf_op jit(solution)/shard_map/ppermute | solution.py:157
  495.1 3.2 copy-start.4
  498.3 9.2 %copy-start.1 = (s32[80,80]{1,0:T(8,128)S(1)}, s32[80,80]{1,0:T(8,128)}, u32[]{:S(2)}) copy-start(s32[80,80]{1,0:T(8,128)} %param.8) | copy-start | bytes 76804
Sparse Core Ops, SparseCore 0:
  9.6 90.7 all-gather.3
  155.2 126.7 all-gather.5
  284.1 126.8 all-gather.7
